TPU v7x, 512 devices: a whole 4x8x8 slice. The times are simulated.
512 devices in a mesh: dp: 32 (over x, y), tp: 16 (over z, core).
Axes of the slice: x: 4, y: 8, z: 8, core: 2. Of those that a mesh axis runs over, the one named last changes fastest.
Arguments:
- embeddings: bfloat16 [12288, 192, 256], P(('dp', 'tp')), may hold values from -6 to 6
- projection: bfloat16 [256, 16], replicated, may hold values from -0.375 to 0.375
- compress: bfloat16 [256, 4], replicated, may hold values from -0.375 to 0.375
- w_up: bfloat16 [4096, 4096], P(None, 'tp'), may hold values from -0.09375 to 0.09375
- w_down: bfloat16 [4096, 768], P('tp'), may hold values from -0.125 to 0.125
- output_norm_gain: float32 [1536], P('tp'), may hold values from 0.25 to 1.75
- out_grad: bfloat16 [12288, 1536], P('dp', 'tp'), may hold values from -6 to 6
Outputs:
- block_result: bfloat16 [12288, 1536], P('dp', 'tp')
- grad_down: float32 [4096, 768], P(('tp', 'dp'))
All inputs are finite; a program needn't handle non-finite values.
Results may differ from a plain program's by a relative error of at most 0.017.
Values may be sent and summed in bfloat16 or wider, within the bound.
No kernel may reach another device: no remote copies, remote signals or barrier semaphores. Data moves between devices by JAX's collectives and lax.ppermute only.
A program may use at most 64 MiB of HBM per device.

v0:
```python
import jax
import jax.numpy as jnp
from jax import lax
from jax.sharding import PartitionSpec as P


def split_up(x, dim, devices):
    before, after = (x.shape[:dim], x.shape[dim + 1 :])
    return jnp.moveaxis(x.reshape(*before, devices, -1, *after), dim, 0)


def summed_on_arrival(x, axis, dim):
    parts = split_up(x, dim, lax.axis_size(axis))
    arrived = lax.all_to_all(parts, axis, split_axis=0, concat_axis=0, tiled=True)
    return arrived.astype(jnp.float32).sum(axis=0)


def sent_to_all(x, axis):
    devices = lax.axis_size(axis)
    return lax.all_to_all(jnp.broadcast_to(x[None], (devices, *x.shape)), axis, 0, 0, tiled=True)


def gathered_once(x, axis):
    leaves = jax.tree.leaves(x)
    sequence = sorted(range(len(leaves)), key=lambda k: -leaves[k].size)
    width = (1, *leaves[sequence[0]].shape)[-1]
    lines = [
        jnp.pad(leaves[k].reshape(-1), (0, -leaves[k].size % width)).reshape(-1, width)
        for k in sequence
    ]
    both, at, found = (sent_to_all(jnp.concatenate(lines), axis), 0, {})
    for k, line in zip(sequence, lines):
        share = both[:, at : at + len(line)].reshape(len(both), -1)
        found[k] = share[:, : leaves[k].size].reshape(-1, *leaves[k].shape)
        at += len(line)
    numbers = iter(range(len(leaves)))
    return jax.tree.map(lambda _: found[next(numbers)], x)


def joined_by_halves(pieces, combine):
    while len(jax.tree.leaves(pieces)[0]) > 1:
        pieces = jax.vmap(combine)(
            *(jax.tree.map(lambda part: part[side::2], pieces) for side in (0, 1))
        )
    return jax.tree.map(lambda part: part[0], pieces)


def joined_all(x, axis, combine):
    pieces = gathered_once(x, axis)
    return joined_by_halves(pieces, combine)


def turned_gather(arrays, axis, dims):
    turned = [jnp.moveaxis(a, dim, 0) for a, dim in zip(arrays, dims)]
    both = jnp.concatenate([t.reshape(len(t), -1) for t in turned], axis=1)
    filled, at, done = (lax.all_gather(both, axis, axis=0, tiled=True), 0, [])
    for t, dim in zip(turned, dims):
        share = filled[:, at : at + t[0].size].reshape(-1, *t.shape[1:])
        done.append(jnp.moveaxis(share, 0, dim))
        at += t[0].size
    return tuple(done)


def chan_merge(left, right):
    count_a, mean_a, dev_a = left
    count_b, mean_b, dev_b = right
    total = count_a + count_b
    delta = mean_b - mean_a
    row_average = mean_a + delta * (count_b / total)
    dev = dev_a + dev_b + delta * delta * (count_a * count_b / total)
    return (total, row_average, dev)


def on_device(embeddings, projection, compress, w_up, w_down, output_norm_gain, out_grad):
    samples = embeddings.shape[0]
    pairs = jnp.einsum(
        "sef,fk->sek", embeddings, projection, preferred_element_type=jnp.float32
    ).astype(jnp.bfloat16)
    inter = jnp.einsum(
        "sek,sef->skf", pairs, embeddings, preferred_element_type=jnp.float32
    ).reshape(samples, -1)
    center = inter - jnp.mean(inter, axis=1, keepdims=True)
    spread = jnp.mean(center * center, axis=1, keepdims=True)
    normed = (center / jnp.sqrt(spread + 1e-05)).astype(jnp.bfloat16)
    lcb = jnp.einsum(
        "sef,fj->sje", embeddings, compress, preferred_element_type=jnp.float32
    ).reshape(samples, -1)
    hidden = jax.nn.gelu(
        jnp.dot(
            lax.all_gather(normed, "tp", axis=0, tiled=True),
            w_up,
            preferred_element_type=jnp.float32,
        ),
        approximate=True,
    ).astype(jnp.bfloat16)
    group_rows = hidden.shape[0]
    tp_count = lax.axis_size("tp")
    mlp = jnp.dot(hidden, w_down, preferred_element_type=jnp.float32)
    mlp_width = mlp.shape[1]
    full_width = mlp_width + lcb.shape[1]
    width = full_width // tp_count
    mlp_share = summed_on_arrival(mlp.astype(jnp.bfloat16), "tp", 1)
    lcb_share = lax.all_to_all(
        lcb.astype(jnp.bfloat16), "tp", split_axis=1, concat_axis=0, tiled=True
    ).astype(lcb.dtype)
    mixed_rows = jnp.concatenate([mlp_share, lcb_share], axis=1)
    own_mean = jnp.mean(mixed_rows, axis=1)
    own_dev = jnp.sum((mixed_rows - own_mean[:, None]) ** 2, axis=1)
    own_count = jnp.full((), width, jnp.float32)
    total, row_average, dev = joined_all((own_count, own_mean, own_dev), "tp", chan_merge)
    inverse_deviation = 1.0 / jnp.sqrt(dev[:, None] / total + 1e-05)
    centered_rows = (mixed_rows - row_average[:, None]) * inverse_deviation
    block_result = (centered_rows * output_norm_gain).astype(jnp.bfloat16)
    scaled_rows = out_grad.astype(jnp.float32) * output_norm_gain
    entire_scaled_rows, entire_normalized_rows = tuple(
        (
            part.astype(jnp.float32)
            for part in turned_gather(
                (scaled_rows.astype(jnp.bfloat16), centered_rows.astype(jnp.bfloat16)), "tp", (1, 1)
            )
        )
    )
    first_moment = jnp.mean(entire_scaled_rows, axis=1, keepdims=True)
    second_moment = jnp.mean(entire_scaled_rows * entire_normalized_rows, axis=1, keepdims=True)
    mixed_gradient = (
        (entire_scaled_rows - first_moment - entire_normalized_rows * second_moment)
        * inverse_deviation
    ).astype(jnp.bfloat16)
    group_mlp = mlp_width // tp_count
    mlp_grad = mixed_gradient.reshape(group_rows, tp_count, -1)[:, :, :group_mlp].reshape(
        group_rows, -1
    )
    grad_down = summed_on_arrival(
        jnp.einsum("rh,rc->hc", hidden, mlp_grad, preferred_element_type=jnp.float32).astype(
            jnp.bfloat16
        ),
        "dp",
        0,
    )
    return (block_result, grad_down)


def solution(mesh):
    return jax.shard_map(
        on_device,
        mesh=mesh,
        in_specs=(
            P(("dp", "tp"), None, None),
            P(),
            P(),
            P(None, "tp"),
            P("tp", None),
            P("tp"),
            P("dp", "tp"),
        ),
        out_specs=(P("dp", "tp"), P(("tp", "dp"), None)),
        check_vma=False,
    )
```

profile of v0, /device:TPU:8, one launch (start us, length us, event | category | flops | bytes accessed | tf_op | source)
XLA Modules:
  0.0 184.7 jit_solution(13328559922858504637)
XLA Ops:
  7.2 0.0 copy-start
  7.2 0.0 copy-start.3
  7.2 0.0 all-gather.3.cloned.1.call-start
  7.2 1.6 copy-done
  8.8 1.8 fusion.26
  10.7 0.4 multiply_reduce_fusion
  11.1 0.2 copy.26
  11.3 0.8 divide_convert_fusion
  12.1 0.0 all-gather.3.cloned.1.call-update
  12.1 0.0 copy-done.3
  12.1 0.7 fusion.6
  12.9 0.1 convert_element_type.74
  13.0 0.8 reshape.145
  13.8 10.4 %all-to-all-start.1 = ((bf16[16,2,576]{2,1,0:T(2,128)(2,1)}), bf16[16,2,576]{2,1,0:T(2,128)(2,1)S(1)}, u32[]{:S(2)}, u32[]{:S(2)}) async-start(bf16[16,2,576]{2,1,0:T(2,128)(2,1)} %reshape.145), calls=%async_computation.1 | async-start | bytes 81920 | tf_op jit(solution)/shard_map/all_to_all | solution.py:103
  24.2 37.1 %all-gather.3.cloned.1.call-done = bf16[384,4096]{1,0:T(8,128)(2,1)} async-done(((bf16[24,4096]{1,0:T(8,128)(2,1)}), bf16[384,4096]{1,0:T(8,128)(2,1)}) %all-gather.3.cloned.1.call-update) | async-done | bytes 3145744 | tf_op jit(solution)/shard_map/all_gather | solution.py:90
  61.3 0.0 copy-start.6
  61.3 3.6 %fusion.29 = f32[384,256]{1,0:T(8,128)S(1)} fusion(bf16[384,4096]{1,0:T(8,128)(2,1)} %all-gather.3.cloned.1.call-done, bf16[4096,256]{1,0:T(8,128)(2,1)} %param.10), kind=kOutput, calls=%fused_computation.71 | convolution fusion | flops 805306368 | bytes 5636096 | tf_op jit(solution)/shard_map/dot_general | solution.py:89
  64.9 0.0 copy-start.7
  64.9 0.7 copy-done.7
  65.7 0.0 copy-done.6
  65.7 0.4 convolution_convert_fusion
  66.0 0.0 copy-start.4
  66.1 0.0 copy-start.2
  66.1 0.0 copy-start.5
  66.1 1.0 copy.19
  67.1 0.0 all-to-all-done.1
  67.1 4.3 %all-to-all-start = ((bf16[16,384,48]{1,2,0:T(8,128)(2,1)}), bf16[16,384,48]{1,2,0:T(8,128)(2,1)S(1)}, u32[]{:S(2)}, u32[]{:S(2)}) async-start(bf16[16,384,48]{1,2,0:T(8,128)(2,1)} %bitcast.2), calls=%async_computation | async-start | bytes 1179648 | tf_op jit(solution)/shard_map/all_to_all | solution.py:14
  71.4 0.0 all-gather.5.cloned.1.call-start
  71.5 0.1 reshape.146
  71.6 0.1 convert_reduce_fusion.4
  71.8 0.1 reduce_sum.108
  71.9 0.1 reduce_sum.110
  72.0 0.1 copy.21
  72.1 16.6 %all-to-all-done = bf16[16,384,48]{1,2,0:T(8,128)(2,1)S(1)} async-done(((bf16[16,384,48]{1,2,0:T(8,128)(2,1)}), bf16[16,384,48]{1,2,0:T(8,128)(2,1)S(1)}, u32[]{:S(2)}, u32[]{:S(2)}) %all-to-all-start) | async-done | bytes 589856 | tf_op jit(solution)/shard_map/all_to_all | solution.py:14
  88.7 0.2 convert_reduce_fusion.1
  88.9 0.0 copy-done.4
  89.0 12.5 %all_to_all.25 = f32[16,3,384]{2,1,0:T(4,128)S(1)} all-to-all(f32[16,3,384]{2,1,0:T(4,128)S(1)} %broadcast_in_dim.2), channel_id=1, replica_groups=mesh['dp'=32,'tp'=16] {'tp'}, dimensions={0} | all-to-all | bytes 147456 | tf_op jit(solution)/shard_map/all_to_all | solution.py:20
  101.5 0.1 fusion.24
  101.7 0.1 slice_reduce_fusion
  101.8 0.1 slice.104
  101.9 0.1 slice.105
  102.0 0.1 slice.108
  102.1 0.1 slice.109
  102.2 0.1 slice.112
  102.3 0.1 slice.113
  102.4 0.6 fusion.25
  105.6 0.1 multiply_add_fusion
  105.8 0.1 multiply_add_fusion.2
  106.6 0.1 multiply_add_fusion.4
  106.8 0.0 copy-done.2
  106.8 0.0 copy-done.5
  106.8 0.7 fusion.16
  107.5 0.7 pad_maximum_fusion.1
  108.2 0.0 all-gather.5.cloned.1.call-update
  108.2 40.1 %all-gather.5.cloned.1.call-done = bf16[1536,768]{1,0:T(8,128)(2,1)} async-done(((bf16[96,768]{1,0:T(8,128)(2,1)}), bf16[1536,768]{1,0:T(8,128)(2,1)}) %all-gather.5.cloned.1.call-update) | async-done | bytes 2359312 | tf_op jit(solution)/shard_map/all_gather | solution.py:56
  148.3 0.0 copy-start.1
  148.3 2.2 %convert_reduce_fusion = (f32[384]{0:T(512)S(1)}, f32[384]{0:T(512)S(1)}) fusion(bf16[1536,768]{1,0:T(8,128)(2,1)} %all-gather.5.cloned.1.call-done), kind=kLoop, calls=%fused_computation.2 | loop fusion | flops 2948352 | bytes 2362368 | tf_op jit(solution)/shard_map/reduce_sum | solution.py:123
  150.6 0.1 copy-done.1
  150.7 0.5 fusion.2
  151.2 0.1 slice.140
  151.3 0.4 copy-done.8
  151.7 0.5 fusion.4
  152.2 25.1 %all_to_all.26 = bf16[32,8,768]{2,1,0:T(8,128)(2,1)S(1)} all-to-all(bf16[32,8,768]{2,1,0:T(8,128)(2,1)S(1)} %fusion.4), channel_id=1, replica_groups=mesh['dp'=32,'tp'=16] {'dp'}, dimensions={0} | all-to-all | bytes 786432 | tf_op jit(solution)/shard_map/all_to_all | solution.py:14
  177.2 0.7 convert_reduce_fusion.3
  (34 shorter events, 0.5 us)
Async XLA Ops:
  7.2 1.7 copy-start
  7.2 5.0 %copy-start.3 = (bf16[256,4]{0,1:T(4,128)(2,1)S(1)}, bf16[256,4]{0,1:T(4,128)(2,1)}, u32[]{:S(2)}) copy-start(bf16[256,4]{0,1:T(4,128)(2,1)} %param.9) | copy-start | bytes 6148
  7.2 54.2 %all-gather.3.cloned.1.call-start = ((), (), s32[]{:S(2)}) async-start(), calls=%async_computation.4 | async-start | bytes 3342336 | tf_op jit(solution)/shard_map/all_gather | solution.py:90
  13.8 53.3 %all-to-all-start.1 = ((bf16[16,2,576]{2,1,0:T(2,128)(2,1)}), bf16[16,2,576]{2,1,0:T(2,128)(2,1)S(1)}, u32[]{:S(2)}, u32[]{:S(2)}) async-start(bf16[16,2,576]{2,1,0:T(2,128)(2,1)} %reshape.145), calls=%async_computation.1 | async-start | bytes 81920 | tf_op jit(solution)/shard_map/all_to_all | solution.py:103
  61.3 4.3 %copy-start.6 = (bf16[256,768]{1,0:T(8,128)(2,1)S(1)}, bf16[256,768]{1,0:T(8,128)(2,1)}, u32[]{:S(2)}) copy-start(bf16[256,768]{1,0:T(8,128)(2,1)} %param.11) | copy-start | bytes 1179652
  64.9 0.7 copy-start.7
  66.0 22.9 %copy-start.4 = (f32[1,384]{1,0:T(1,128)S(1)}, f32[1,384]{1,0:T(1,128)}, u32[]{:S(2)}) copy-start(f32[1,384]{1,0:T(1,128)} %constant.29.clone.1) | copy-start | bytes 4612
  66.1 40.7 %copy-start.2 = (bf16[384,96]{0,1:T(8,128)(2,1)S(1)}, bf16[384,96]{0,1:T(8,128)(2,1)}, u32[]{:S(2)}) copy-start(bf16[384,96]{0,1:T(8,128)(2,1)} %param.13) | copy-start | bytes 221188
  66.1 40.7 %copy-start.5 = (f32[96]{0:T(128)S(1)}, f32[96]{0:T(128)}, u32[]{:S(2)}) copy-start(f32[96]{0:T(128)} %param.12) | copy-start | bytes 1156
  67.1 21.5 %all-to-all-start = ((bf16[16,384,48]{1,2,0:T(8,128)(2,1)}), bf16[16,384,48]{1,2,0:T(8,128)(2,1)S(1)}, u32[]{:S(2)}, u32[]{:S(2)}) async-start(bf16[16,384,48]{1,2,0:T(8,128)(2,1)} %bitcast.2), calls=%async_computation | async-start | bytes 1179648 | tf_op jit(solution)/shard_map/all_to_all | solution.py:14
  71.4 76.9 %all-gather.5.cloned.1.call-start = ((), (), s32[]{:S(2)}) async-start(), calls=%async_computation.5 | async-start | bytes 2506752 | tf_op jit(solution)/shard_map/all_gather | solution.py:56
  148.3 2.4 %copy-start.1 = (bf16[1536,768]{1,0:T(8,128)(2,1)S(1)}, bf16[1536,768]{1,0:T(8,128)(2,1)}, u32[]{:S(2)}) copy-start(bf16[1536,768]{1,0:T(8,128)(2,1)} %all-gather.5.cloned.1.call-done) | copy-start | bytes 7077892
  150.7 1.0 copy-start.8
Sparse Core Ops, SparseCore 0:
  12.3 49.0 all-gather.2
  108.3 39.9 all-gather.4
where the time goes:
time: 185 us
  waiting for transfers between devices  93.8 us (51%)
  blocking collectives  37.6 us (20%)
  between operations  17.6 us (10%)
  starting transfers between devices  14.8 us (8%)
  local copies, waits for them, and re-layouts  7.2 us (4%)
  matrix products  6.93 us (4%)
  other arithmetic  6.77 us (4%)
    all_gather x1, waiting for transfers between devices, turned_gather(): filled, at, done = (lax.all_gather(both, axis, axis=0, tiled=True), 0, [])  40.1 us
    all_gather x1, waiting for transfers between devices, on_device(): lax.all_gather(normed, 'tp', axis=0, tiled=True)  37.1 us
    all_to_all x1, blocking collectives, summed_on_arrival(): lax.all_to_all(parts, axis, split_axis=0, concat_axis=0, tiled=True)  25.1 us
    all_to_all x1, waiting for transfers between devices, summed_on_arrival(): lax.all_to_all(parts, axis, split_axis=0, concat_axis=0, tiled=True)  16.6 us
    all_to_all x1, blocking collectives, sent_to_all(): lax.all_to_all(jnp.broadcast_to(x[None], (devices, *x.shape)), axis, 0, 0...  12.5 us
    all_to_all x1, starting transfers between devices, on_device(): lax.all_to_all(lcb.astype(jnp.bfloat16), 'tp', split_axis=1, concat_axis=...  10.4 us
    all_to_all x1, starting transfers between devices, summed_on_arrival(): lax.all_to_all(parts, axis, split_axis=0, concat_axis=0, tiled=True)  4.3 us
    unnamed x22, local copies, waits for them, and re-layouts  4.06 us
  transfers between devices with their start and end apart: 4, of which 3 were waited for; matrix products, arithmetic and copies ran while one was open for 4% of the time, Pallas kernels for 0%

commit v1 on v0

--- a/solution.py
+++ b/solution.py
@@ -53,7 +53,13 @@
 def turned_gather(arrays, axis, dims):
     turned = [jnp.moveaxis(a, dim, 0) for a, dim in zip(arrays, dims)]
     both = jnp.concatenate([t.reshape(len(t), -1) for t in turned], axis=1)
-    filled, at, done = (lax.all_gather(both, axis, axis=0, tiled=True), 0, [])
+    filled, at, done = (
+        jnp.concatenate(
+            lax.all_to_all(jnp.stack([both] * lax.axis_size(axis)), axis, 0, 0), axis=0
+        ),
+        0,
+        [],
+    )
     for t, dim in zip(turned, dims):
         share = filled[:, at : at + t[0].size].reshape(-1, *t.shape[1:])
         done.append(jnp.moveaxis(share, 0, dim))

time: 185 us -> 202 us (1.092)
  blocking collectives: 37.6 us -> 96.7 us
  waiting for transfers between devices: 93.8 us -> 53.7 us
  other arithmetic: 6.77 us -> 4.33 us
    all_to_all x0 -> x1, blocking collectives: none -> 58.7 us  [turned_gather(): lax.all_to_all(jnp.stack([both] * lax.axis_size(axis)), axis, 0, 0)]
    all_gather x1 -> x0, waiting for transfers between devices: 40.1 us -> none  [turned_gather(): filled, at, done = (lax.all_gather(both, axis, axis=0, tiled=True), 0, [])]
    unnamed x22 -> x20, local copies, waits for them, and re-layouts: 4.06 us -> 3.93 us
  transfers between devices with their start and end apart: 4 -> 3, of which waited for: 3 -> 2; matrix products, arithmetic and copies ran while one was open for 4% -> 4% of each run, Pallas kernels for 0% -> 0%
where the time goes in v1:
time: 202 us; the launch traced here: 201 us
  blocking collectives  96.7 us (48%)
  waiting for transfers between devices  53.7 us (27%)
  between operations  17.6 us (9%)
  starting transfers between devices  14.8 us (7%)
  local copies, waits for them, and re-layouts  7.31 us (4%)
  matrix products  6.93 us (3%)
  other arithmetic  4.33 us (2%)
    all_to_all x1, blocking collectives, turned_gather(): lax.all_to_all(jnp.stack([both] * lax.axis_size(axis)), axis, 0, 0)  58.7 us
    all_gather x1, waiting for transfers between devices, on_device(): lax.all_gather(normed, 'tp', axis=0, tiled=True)  37.1 us
    all_to_all x1, blocking collectives, summed_on_arrival(): lax.all_to_all(parts, axis, split_axis=0, concat_axis=0, tiled=True)  25.5 us
    all_to_all x1, waiting for transfers between devices, summed_on_arrival(): lax.all_to_all(parts, axis, split_axis=0, concat_axis=0, tiled=True)  16.6 us
    all_to_all x1, blocking collectives, sent_to_all(): lax.all_to_all(jnp.broadcast_to(x[None], (devices, *x.shape)), axis, 0, 0...  12.5 us
    all_to_all x1, starting transfers between devices, on_device(): lax.all_to_all(lcb.astype(jnp.bfloat16), 'tp', split_axis=1, concat_axis=...  10.4 us
    all_to_all x1, starting transfers between devices, summed_on_arrival(): lax.all_to_all(parts, axis, split_axis=0, concat_axis=0, tiled=True)  4.3 us
  transfers between devices with their start and end apart: 3, of which 2 were waited for; matrix products, arithmetic and copies ran while one was open for 4% of the time, Pallas kernels for 0%

profile of v1, /device:TPU:8, one launch (start us, length us, event | category | flops | bytes accessed | tf_op | source)
XLA Modules:
  0.0 201.4 jit_solution(371226531162347347)
XLA Ops:
  7.2 0.0 copy-start
  7.2 0.0 copy-start.2
  7.2 0.0 all-gather.2.cloned.1.call-start
  7.2 1.6 copy-done
  8.8 1.8 fusion.26
  10.7 0.4 multiply_reduce_fusion
  11.1 0.2 copy.31
  11.3 0.8 divide_convert_fusion
  12.1 0.0 all-gather.2.cloned.1.call-update
  12.1 0.0 copy-done.2
  12.1 0.7 fusion.6
  12.9 0.1 convert_element_type.74
  13.0 0.8 reshape.151
  13.8 10.4 %all-to-all-start.1 = ((bf16[16,2,576]{2,1,0:T(2,128)(2,1)}), bf16[16,2,576]{2,1,0:T(2,128)(2,1)S(1)}, u32[]{:S(2)}, u32[]{:S(2)}) async-start(bf16[16,2,576]{2,1,0:T(2,128)(2,1)} %reshape.151), calls=%async_computation.1 | async-start | bytes 81920 | tf_op jit(solution)/shard_map/all_to_all | solution.py:109
  24.2 37.1 %all-gather.2.cloned.1.call-done = bf16[384,4096]{1,0:T(8,128)(2,1)} async-done(((bf16[24,4096]{1,0:T(8,128)(2,1)}), bf16[384,4096]{1,0:T(8,128)(2,1)}) %all-gather.2.cloned.1.call-update) | async-done | bytes 3145744 | tf_op jit(solution)/shard_map/all_gather | solution.py:96
  61.3 0.0 copy-start.5
  61.3 3.6 %fusion.29 = f32[384,256]{1,0:T(8,128)S(1)} fusion(bf16[384,4096]{1,0:T(8,128)(2,1)} %all-gather.2.cloned.1.call-done, bf16[4096,256]{1,0:T(8,128)(2,1)} %param.10), kind=kOutput, calls=%fused_computation.71 | convolution fusion | flops 805306368 | bytes 5636096 | tf_op jit(solution)/shard_map/dot_general | solution.py:95
  64.9 0.0 copy-start.6
  64.9 0.7 copy-done.6
  65.7 0.0 copy-done.5
  65.7 0.4 convolution_convert_fusion
  66.0 0.0 copy-start.3
  66.1 0.0 copy-start.1
  66.1 0.0 copy-start.4
  66.1 1.0 copy.24
  67.1 0.0 all-to-all-done.1
  67.1 4.3 %all-to-all-start = ((bf16[16,384,48]{1,2,0:T(8,128)(2,1)}), bf16[16,384,48]{1,2,0:T(8,128)(2,1)S(1)}, u32[]{:S(2)}, u32[]{:S(2)}) async-start(bf16[16,384,48]{1,2,0:T(8,128)(2,1)} %bitcast.2), calls=%async_computation | async-start | bytes 1179648 | tf_op jit(solution)/shard_map/all_to_all | solution.py:14
  71.4 0.1 reshape.152
  71.6 0.1 convert_reduce_fusion.4
  71.7 0.1 reduce_sum.108
  71.8 0.1 reduce_sum.110
  71.9 0.1 copy.26
  72.0 16.6 %all-to-all-done = bf16[16,384,48]{1,2,0:T(8,128)(2,1)S(1)} async-done(((bf16[16,384,48]{1,2,0:T(8,128)(2,1)}), bf16[16,384,48]{1,2,0:T(8,128)(2,1)S(1)}, u32[]{:S(2)}, u32[]{:S(2)}) %all-to-all-start) | async-done | bytes 589856 | tf_op jit(solution)/shard_map/all_to_all | solution.py:14
  88.7 0.2 convert_reduce_fusion.1
  88.9 0.0 copy-done.3
  89.0 12.5 %all_to_all.30 = f32[16,3,384]{2,1,0:T(4,128)S(1)} all-to-all(f32[16,3,384]{2,1,0:T(4,128)S(1)} %broadcast_in_dim.2), channel_id=1, replica_groups=mesh['dp'=32,'tp'=16] {'tp'}, dimensions={0} | all-to-all | bytes 147456 | tf_op jit(solution)/shard_map/all_to_all | solution.py:20
  101.5 0.1 fusion.24
  101.7 0.1 slice_reduce_fusion
  101.8 0.1 slice.104
  101.9 0.1 slice.105
  102.0 0.1 slice.108
  102.1 0.1 slice.109
  102.2 0.1 slice.112
  102.3 0.1 slice.113
  102.4 0.6 fusion.25
  105.6 0.1 multiply_add_fusion
  105.8 0.1 multiply_add_fusion.2
  106.6 0.1 multiply_add_fusion.4
  106.8 0.0 copy-done.1
  106.8 0.0 copy-done.4
  106.8 0.7 fusion.16
  107.5 0.2 stack.2
  107.8 58.7 %all_to_all.31 = bf16[16,96,768]{2,1,0:T(8,128)(2,1)S(1)} all-to-all(bf16[16,96,768]{2,1,0:T(8,128)(2,1)S(1)} %stack.2), channel_id=1, replica_groups=mesh['dp'=32,'tp'=16] {'tp'}, dimensions={0} | all-to-all | bytes 4718592 | tf_op jit(solution)/shard_map/all_to_all | solution.py:58
  166.5 0.5 convert_reduce_fusion
  166.9 0.0 copy-start.7
  166.9 0.5 fusion.2
  167.5 0.1 slice.140
  167.5 0.4 copy-done.7
  167.9 0.5 fusion.4
  168.4 25.5 %all_to_all.32 = bf16[32,8,768]{2,1,0:T(8,128)(2,1)S(1)} all-to-all(bf16[32,8,768]{2,1,0:T(8,128)(2,1)S(1)} %fusion.4), channel_id=1, replica_groups=mesh['dp'=32,'tp'=16] {'dp'}, dimensions={0} | all-to-all | bytes 786432 | tf_op jit(solution)/shard_map/all_to_all | solution.py:14
  193.9 0.7 convert_reduce_fusion.3
  (34 shorter events, 0.5 us)
Async XLA Ops:
  7.2 1.7 copy-start
  7.2 5.0 %copy-start.2 = (bf16[256,4]{0,1:T(4,128)(2,1)S(1)}, bf16[256,4]{0,1:T(4,128)(2,1)}, u32[]{:S(2)}) copy-start(bf16[256,4]{0,1:T(4,128)(2,1)} %param.9) | copy-start | bytes 6148
  7.2 54.2 %all-gather.2.cloned.1.call-start = ((), (), s32[]{:S(2)}) async-start(), calls=%async_computation.5 | async-start | bytes 3342336 | tf_op jit(solution)/shard_map/all_gather | solution.py:96
  13.8 53.3 %all-to-all-start.1 = ((bf16[16,2,576]{2,1,0:T(2,128)(2,1)}), bf16[16,2,576]{2,1,0:T(2,128)(2,1)S(1)}, u32[]{:S(2)}, u32[]{:S(2)}) async-start(bf16[16,2,576]{2,1,0:T(2,128)(2,1)} %reshape.151), calls=%async_computation.1 | async-start | bytes 81920 | tf_op jit(solution)/shard_map/all_to_all | solution.py:109
  61.3 4.3 %copy-start.5 = (bf16[256,768]{1,0:T(8,128)(2,1)S(1)}, bf16[256,768]{1,0:T(8,128)(2,1)}, u32[]{:S(2)}) copy-start(bf16[256,768]{1,0:T(8,128)(2,1)} %param.11) | copy-start | bytes 1179652
  64.9 0.7 copy-start.6
  66.0 22.9 %copy-start.3 = (f32[1,384]{1,0:T(1,128)S(1)}, f32[1,384]{1,0:T(1,128)}, u32[]{:S(2)}) copy-start(f32[1,384]{1,0:T(1,128)} %constant.29.clone.1) | copy-start | bytes 4612
  66.1 40.7 %copy-start.1 = (bf16[384,96]{0,1:T(8,128)(2,1)S(1)}, bf16[384,96]{0,1:T(8,128)(2,1)}, u32[]{:S(2)}) copy-start(bf16[384,96]{0,1:T(8,128)(2,1)} %param.13) | copy-start | bytes 221188
  66.1 40.7 %copy-start.4 = (f32[96]{0:T(128)S(1)}, f32[96]{0:T(128)}, u32[]{:S(2)}) copy-start(f32[96]{0:T(128)} %param.12) | copy-start | bytes 1156
  67.1 21.5 %all-to-all-start = ((bf16[16,384,48]{1,2,0:T(8,128)(2,1)}), bf16[16,384,48]{1,2,0:T(8,128)(2,1)S(1)}, u32[]{:S(2)}, u32[]{:S(2)}) async-start(bf16[16,384,48]{1,2,0:T(8,128)(2,1)} %bitcast.2), calls=%async_computation | async-start | bytes 1179648 | tf_op jit(solution)/shard_map/all_to_all | solution.py:14
  166.9 1.0 copy-start.7
Sparse Core Ops, SparseCore 0:
  12.3 49.0 all-gather.1
